TPU v7x, 32 devices: a whole 2x2x4 slice. The times are simulated.
32 devices in a mesh: member: 4 (over y, core), region: 8 (over z, x).
Axes of the slice: x: 2, y: 2, z: 4, core: 2. Of those that a mesh axis runs over, the one named last changes fastest.
Arguments:
- latent: bfloat16 [8, 1024, 1024], P('member', 'region'), may hold values from -6 to 6
- w_node: bfloat16 [1024, 1024], replicated, may hold values from -0.1875 to 0.1875
- bias: float32 [1024], replicated, may hold values from -3 to 3
- w_out: bfloat16 [100, 1024], replicated, may hold values from -0.1875 to 0.1875
- edge_src: int32 [16384, 3], P('region'), may hold values from 0 to 383
- edge_weight: float32 [16384, 3], P('region'), may hold values from 0.2 to 0.6
- target: float32 [100, 16384], P(None, 'region'), may hold values from -6 to 6
- area: float32 [16384], P('region'), may hold values from 0.3 to 30
Outputs:
- grad_node: float32 [1024, 1024], P('region')
- grad_out: float32 [100, 1024], replicated
- grad_bias: float32 [1024], replicated
- loss: float32 [8], P('region')
Inputs may be any that keep to these rules, and one draw needn't show every extreme that they name: `edge_src`: an index into the latent nodes of the previous region, then the grid point's own region, then the next region, 128 each; regions form a loop.
All inputs are finite; a program needn't handle non-finite values.
Results may differ from a plain program's by a relative error of at most 0.007.
Values may be sent and summed in bfloat16 or wider, within the bound.
A program may use at most 128 MiB of HBM per device.

v0:
```python
import jax
import jax.numpy as jnp
from jax import lax
from jax.sharding import PartitionSpec as P

smooth_sq = 0.01
smooth_width = 0.1


def padded(block, sides, width):
    for axis, dim in sides:
        count = lax.axis_size(axis)
        forward = [(i, i + 1) for i in range(count - 1)]
        forward.append((count - 1, 0))
        backward = [(target, source) for source, target in forward]
        low = lax.ppermute(
            lax.slice_in_dim(block, block.shape[dim] - width, None, axis=dim), axis, forward
        )
        high = lax.ppermute(lax.slice_in_dim(block, 0, width, axis=dim), axis, backward)
        block = jnp.concatenate([low, block, high], axis=dim)
    return block


def passed_along(value, axis, steps):
    count = lax.axis_size(axis)
    pairs = [(source, (source + steps) % count) for source in range(count)]
    return lax.ppermute(value, axis, pairs)


def gelu_slope(values):
    inner = 0.7978845608028654 * (values + 0.044715 * values * values * values)
    tanh_part = jnp.tanh(inner)
    return 0.5 * (1.0 + tanh_part) + 0.5 * values * (
        1.0 - tanh_part * tanh_part
    ) * 0.7978845608028654 * (1.0 + 3.0 * 0.044715 * values * values)


def contract_rows(left, right):
    return lax.dot_general(
        left, right, (((0,), (0,)), ((), ())), preferred_element_type=jnp.float32
    )


def local(latent, w_node, bias, w_out, edge_src, edge_weight, target, area):
    members_here, nodes, width = latent.shape
    points, fanout = edge_src.shape
    variables = target.shape[0]
    positions = lax.broadcasted_iota(jnp.int32, (points, 3 * nodes), 1)
    adjacency = jnp.zeros((points, 3 * nodes), jnp.float32)
    for slot in range(fanout):
        adjacency = adjacency + jnp.where(
            edge_src[:, slot][:, None] == positions, edge_weight[:, slot][:, None], 0.0
        )
    adj_high = adjacency.astype(jnp.bfloat16)
    adj_low = (adjacency - adj_high.astype(jnp.float32)).astype(jnp.bfloat16)
    proj = jnp.einsum("mnh,hk->mnk", latent, w_node, preferred_element_type=jnp.float32).astype(
        jnp.bfloat16
    )
    extended = padded(proj, (("region", 1),), nodes)
    pre = bias[None, None, :] + jnp.einsum(
        "gj,mjh->mgh", adj_high, extended, preferred_element_type=jnp.float32
    )
    pre = pre + jnp.einsum("gj,mjh->mgh", adj_low, extended, preferred_element_type=jnp.float32)
    hidden = jax.nn.gelu(pre, approximate=True).astype(jnp.bfloat16)
    preds = jnp.einsum("vh,mgh->mvg", w_out, hidden, preferred_element_type=jnp.float32)
    errors = preds - target[None]
    count = members_here * lax.axis_size("member")
    quarter = points // lax.axis_size("member")
    block = lax.all_to_all(errors, "member", split_axis=2, concat_axis=0, tiled=True)
    own = jnp.sqrt(block * block + smooth_sq)
    diff = block[:, None] - block[None]
    dist = jnp.sqrt(diff * diff + smooth_sq)
    pair_total = jnp.sum(dist, axis=(0, 1)) - count * smooth_width
    crps_point = jnp.mean(own, 0) - pair_total / (2.0 * count * (count - 1))
    bracket_here = block / own / count - jnp.sum(diff / dist, axis=1) / (count * (count - 1))
    returned = lax.all_to_all(bracket_here, "member", split_axis=0, concat_axis=2, tiled=True)
    crps_block = crps_point[None]
    area_part = lax.dynamic_slice_in_dim(area, lax.axis_index("member") * quarter, quarter, 0)
    loss_part = jnp.sum(crps_block[0] * area_part[None, :])
    dpred = (returned * (area / variables)[None, None, :]).astype(jnp.bfloat16)
    grad_out_local = jnp.einsum("mvg,mgh->vh", dpred, hidden, preferred_element_type=jnp.float32)
    dhidden = jnp.einsum("mvg,vh->mgh", dpred, w_out, preferred_element_type=jnp.float32)
    dpre = (dhidden * gelu_slope(pre)).astype(jnp.bfloat16)
    bias_local = jnp.sum(dpre.astype(jnp.float32), axis=(0, 1))
    contrib = jnp.einsum("gj,mgh->mjh", adj_high, dpre, preferred_element_type=jnp.float32)
    contrib = contrib + jnp.einsum("gj,mgh->mjh", adj_low, dpre, preferred_element_type=jnp.float32)
    rounded = contrib.astype(jnp.bfloat16)
    head = lax.psum((loss_part / variables, grad_out_local, bias_local), "member")
    region_heads = lax.psum((head[1], head[2]), "region")
    loss = (head[0] / points).reshape(1)
    from_next = passed_along(rounded[:, :nodes], "region", -1)
    from_prior = passed_along(rounded[:, 2 * nodes :], "region", 1)
    latent_flat = latent.reshape(members_here * nodes, width)
    pairings = [
        (latent_flat, rounded[:, nodes : 2 * nodes].reshape(members_here * nodes, width)),
        (latent_flat, from_next.reshape(members_here * nodes, width)),
        (latent_flat, from_prior.reshape(members_here * nodes, width)),
    ]
    total = jnp.zeros((width, width), jnp.float32)
    for left, right in pairings:
        total = total + contract_rows(left, right)
    summed = lax.psum(total, "member")
    grad_node = lax.psum_scatter(summed, "region", scatter_dimension=0, tiled=True)
    return (grad_node, region_heads[0], region_heads[1], loss)


def solution(mesh):
    return jax.shard_map(
        local,
        mesh=mesh,
        in_specs=(
            P("member", "region", None),
            P(),
            P(),
            P(),
            P("region", None),
            P("region", None),
            P(None, "region"),
            P("region"),
        ),
        out_specs=(P("region", None), P(), P(), P("region")),
        check_vma=False,
    )
```

profile of v0, /device:TPU:0, one launch (start us, length us, event | category | flops | bytes accessed | tf_op | source)
XLA Modules:
  0.0 436.7 jit_solution(2896631980654819759)
XLA Ops:
  7.2 1.6 copy-done
  8.8 1.7 fusion.32
  10.5 6.0 %collective-permute-start.1 = (bf16[2,128,1024]{2,1,0:T(8,128)(2,1)S(1)}, bf16[2,128,1024]{2,1,0:T(8,128)(2,1)S(1)}, u32[]{:S(2)}, u32[]{:S(2)}) collective-permute-start(bf16[2,128,1024]{2,1,0:T(8,128)(2,1)S(1)} %fusion.32), channel_id=1, source_target_pairs={{1,0},{2,1},{3,2},{4,3},{5,4},{6,5},{7,6},{0,7},{9,8},{10,9},{11,1... | collective-permute-start | bytes 1572872 | tf_op jit(solution)/shard_map/ppermute | solution.py:19
  16.6 20.1 %collective-permute-done.1 = bf16[2,128,1024]{2,1,0:T(8,128)(2,1)S(1)} collective-permute-done((bf16[2,128,1024]{2,1,0:T(8,128)(2,1)S(1)}, bf16[2,128,1024]{2,1,0:T(8,128)(2,1)S(1)}, u32[]{:S(2)}, u32[]{:S(2)}) %collective-permute-start.1) | collective-permute-done | bytes 524320 | tf_op jit(solution)/shard_map/ppermute | solution.py:19
  36.8 9.2 %fusion.29 = f32[2,1024,2048]{2,1,0:T(8,128)} fusion(bf16[2,128,1024]{2,1,0:T(8,128)(2,1)S(1)} %collective-permute-done.1, bf16[2,128,1024]{2,1,0:T(8,128)(2,1)S(1)} %fusion.32, bf16[2,128,1024]{2,1,0:T(8,128)(2,1)S(1)} %collective-permute-done, f32[2048]{0:T(1024)S(1)} %bitcast.102, s32[2048]{0:T(1024)S(1)} %bitcast.90, f32[2048]{0:T(1024)S(1)} %bitcast.106, ...), kind=kOutput, calls=%fused_computation.50 | convolution fusion | flops 3233021952 | bytes 18399232 | tf_op jit(solution)/shard_map/gj,mjh->mgh/dot_general | solution.py:60
  46.1 19.5 %fusion.7 = (bf16[2,2048,1024]{1,2,0:T(8,128)(2,1)}, f32[2,1024,2048]{2,1,0:T(8,128)}) fusion(f32[2,1024,2048]{2,1,0:T(8,128)} %fusion.29, f32[1024]{0:T(1024)S(1)} %copy-done.9, f32[2048]{0:T(1024)S(1)} %bitcast.103, s32[2048]{0:T(1024)S(1)} %bitcast.91, f32[2048]{0:T(1024)S(1)} %bitcast.107, s32[2048]{0:T(1024)S(1)} %bitcast.95, f32[2048]{0:T(1024)S(1)} %bitcast.99, ...), kind=kOutput, calls=%fused_computation.12 | convolution fusion | flops 3281518592 | bytes 43569152 | tf_op jit(solution)/shard_map/gj,mjh->mgh/dot_general | solution.py:63
  65.6 4.8 %fusion.23 = f32[2,100,2048]{2,1,0:T(8,128)S(1)} fusion(bf16[2,2048,1024]{1,2,0:T(8,128)(2,1)} %get-tuple-element.34, f32[100,2048]{1,0:T(8,128)S(1)} %copy-done.2, bf16[100,1024]{1,0:T(8,128)(2,1)S(1)} %copy-done.5), kind=kOutput, calls=%fused_computation.40 | convolution fusion | flops 839270400 | bytes 11051008 | tf_op jit(solution)/shard_map/vh,mgh->mvg/dot_general | solution.py:65
  70.4 2.4 copy.39
  72.8 29.6 %all_to_all.36 = f32[2,100,2048]{1,0,2:T(2,128)S(1)} all-to-all(f32[2,100,2048]{1,0,2:T(2,128)} %copy.39), channel_id=1, replica_groups=mesh['member'=4,'region'=8] {'member'}, dimensions={2} | all-to-all | bytes 3276800 | tf_op jit(solution)/shard_map/all_to_all | solution.py:69
  102.4 2.3 copy.52
  104.7 2.0 copy.41
  107.7 23.3 %fusion.19 = (f32[100,512]{1,0:T(8,128)S(1)}, f32[8,100,512]{2,1,0:T(8,128)S(1)}) fusion(f32[8,100,512]{2,0,1:T(8,128)S(1)} %copy.42, f32[8,100,512]{2,1,0:T(8,128)S(1)} %bitcast.82), kind=kLoop, calls=%fused_computation.27 | loop fusion | flops 19200000 | bytes 5120000 | tf_op jit(solution)/shard_map/reduce_sum | solution.py:73
  130.9 1.7 multiply_subtract_fusion
  132.6 3.6 all-to-all-start.1
  136.3 21.4 %all-to-all-done.1 = f32[8,100,512]{2,1,0:T(8,128)S(1)} async-done(((f32[8,100,512]{2,1,0:T(8,128)}), f32[8,100,512]{2,1,0:T(8,128)S(1)}, u32[]{:S(2)}, u32[]{:S(2)}) %all-to-all-start.1) | async-done | bytes 1638432 | tf_op jit(solution)/shard_map/all_to_all | solution.py:76
  157.6 2.2 copy.43
  159.9 2.6 all_to_all.33
  162.4 20.2 %convert_reduce_fusion = (f32[1024]{0:T(1024)S(1)}, bf16[2,2048,1024]{1,2,0:T(8,128)(2,1)}) fusion(f32[2,1024,2048]{2,1,0:T(8,128)} %get-tuple-element.35, f32[2,1024,2048]{2,1,0:T(8,128)} %fusion.29, f32[1024]{0:T(1024)S(1)} %copy-done.9, bf16[100,1024]{1,0:T(8,128)(2,1)S(1)} %copy-done.5, f32[2,100,2048]{2,1,0:T(8,128)S(1)} %all_to_all.33, ...), kind=kOutput, calls=%fused_computation.23 | convolution fusion | flops 936147968 | bytes 43802624 | tf_op jit(solution)/shard_map/mvg,vh->mgh/dot_general | solution.py:82
  182.7 8.4 %fusion.27 = f32[2,1024,384]{2,1,0:T(8,128)S(1)} fusion(bf16[2,2048,1024]{1,2,0:T(8,128)(2,1)} %get-tuple-element.37, f32[2048]{0:T(1024)S(1)} %bitcast.104, s32[2048]{0:T(1024)S(1)} %bitcast.92, f32[2048]{0:T(1024)S(1)} %bitcast.108, s32[2048]{0:T(1024)S(1)} %bitcast.96, f32[2048]{0:T(1024)S(1)} %bitcast.100, s32[2048]{0:T(1024)S(1)} %bitcast.88), kind=kOutput, calls=%fused_computation.48 | convolution fusion | flops 3228303360 | bytes 11583488 | tf_op jit(solution)/shard_map/gj,mgh->mjh/dot_general | solution.py:85
  191.1 5.0 %fusion.31 = bf16[2,384,1024]{1,2,0:T(8,128)(2,1)S(1)} fusion(f32[2,1024,384]{2,1,0:T(8,128)S(1)} %fusion.27, bf16[2,2048,1024]{1,2,0:T(8,128)(2,1)S(1)} %copy-done.10, f32[2048]{0:T(1024)S(1)} %bitcast.105, s32[2048]{0:T(1024)S(1)} %bitcast.93, f32[2048]{0:T(1024)S(1)} %bitcast.109, s32[2048]{0:T(1024)S(1)} %bitcast.97, f32[2048]{0:T(1024)S(1)} %bitcast.101, ...), kind=kOutput, calls=%fused_computation.52 | convolution fusion | flops 3232235520 | bytes 13156352 | tf_op jit(solution)/shard_map/gj,mgh->mjh/dot_general | solution.py:86
  196.3 4.9 %collective-permute-start.2 = (bf16[2,128,1024]{1,2,0:T(8,128)(2,1)S(1)}, bf16[2,128,1024]{1,2,0:T(8,128)(2,1)S(1)}, u32[]{:S(2)}, u32[]{:S(2)}) collective-permute-start(bf16[2,128,1024]{1,2,0:T(8,128)(2,1)S(1)} %get-tuple-element.27), channel_id=1, source_target_pairs={{0,7},{1,0},{2,1},{3,2},{4,3},{5,4},{6,5},{7,6},{8,15},{9,8},{10,9... | collective-permute-start | bytes 1572872 | tf_op jit(solution)/shard_map/ppermute | solution.py:27
  202.0 19.9 %collective-permute-done.2 = bf16[2,128,1024]{1,2,0:T(8,128)(2,1)S(1)} collective-permute-done((bf16[2,128,1024]{1,2,0:T(8,128)(2,1)S(1)}, bf16[2,128,1024]{1,2,0:T(8,128)(2,1)S(1)}, u32[]{:S(2)}, u32[]{:S(2)}) %collective-permute-start.2) | collective-permute-done | bytes 524320 | tf_op jit(solution)/shard_map/ppermute | solution.py:27
  222.6 2.7 fusion.21
  225.5 7.5 %convolution_bitcast_fusion.1 = f32[100,1024]{1,0:T(8,128)} fusion(bf16[2,2048,1024]{1,2,0:T(8,128)(2,1)} %get-tuple-element.34, f32[2,100,2048]{2,1,0:T(8,128)} %copy-done.3, f32[2048]{0:T(1024)S(1)} %broadcast_multiply_fusion), kind=kOutput, calls=%fused_computation.54 | convolution fusion | flops 839680000 | bytes 10444800 | tf_op jit(solution)/shard_map/mvg,mgh->vh/dot_general | solution.py:81
  233.0 80.0 %reduce-scatter.2.cloned.1.call-done = f32[128,1024]{0,1:T(8,128)} async-done(((f32[1024,1024]{0,1:T(8,128)}), f32[128,1024]{0,1:T(8,128)}) %reduce-scatter.2.cloned.1.call-update) | async-done | bytes 524304 | tf_op jit(solution)/shard_map/reduce_scatter | solution.py:103
  313.1 38.6 %all-reduce.7.cloned.1.call-done = (f32[128,1024]{0,1:T(8,128)}, f32[100,1024]{1,0:T(8,128)}) async-done(((f32[128,1024]{0,1:T(8,128)}, f32[100,1024]{1,0:T(8,128)}), (f32[128,1024]{0,1:T(8,128)}, f32[100,1024]{1,0:T(8,128)})) %all-reduce.7.cloned.1.call-update) | async-done | bytes 933904 | tf_op jit(solution)/shard_map/psum | solution.py:102
  351.7 3.4 sqrt_reduce_fusion
  356.5 6.3 %all-reduce = (f32[1024]{0:T(1024)S(1)}, f32[]{:T(128)}) all-reduce(f32[1024]{0:T(1024)S(1)} %get-tuple-element.36, f32[]{:T(128)S(6)} %div.54), channel_id=1, replica_groups=mesh['member'=4,'region'=8] {'member'}, use_global_device_ids=true, to_apply=%region_6.7 | all-reduce | flops 1025 | bytes 8200 | tf_op jit(solution)/shard_map/psum | solution.py:88
  363.5 22.1 %psum.46 = f32[1024]{0:T(1024)} all-reduce(f32[1024]{0:T(1024)S(1)} %get-tuple-element.22), channel_id=1, replica_groups=mesh['member'=4,'region'=8] {'region'}, use_global_device_ids=true, to_apply=%region_7.8 | all-reduce | flops 1024 | bytes 8192 | tf_op jit(solution)/shard_map/psum | solution.py:89
  385.5 2.0 copy.46
  387.6 39.5 %all-reduce.5.cloned.1.call-done = f32[100,1024]{1,0:T(8,128)} async-done(((f32[100,1024]{1,0:T(8,128)}), f32[100,1024]{1,0:T(8,128)}) %all-reduce.5.cloned.1.call-update) | async-done | bytes 409616 | tf_op jit(solution)/shard_map/psum | solution.py:89
  427.0 1.8 copy.56
  (40 shorter events, 3.9 us)
Async XLA Ops:
  7.2 1.6 copy-start
  7.2 9.4 %copy-start.6 = (s32[2048,3]{0,1:T(4,128)S(1)}, s32[2048,3]{0,1:T(4,128)}, u32[]{:S(2)}) copy-start(s32[2048,3]{0,1:T(4,128)} %param.12) | copy-start | bytes 73732
  7.2 9.4 %copy-start.7 = (f32[2048,3]{0,1:T(4,128)S(1)}, f32[2048,3]{0,1:T(4,128)}, u32[]{:S(2)}) copy-start(f32[2048,3]{0,1:T(4,128)} %param.13) | copy-start | bytes 73732
  10.5 26.1 %collective-permute-start.1 = (bf16[2,128,1024]{2,1,0:T(8,128)(2,1)S(1)}, bf16[2,128,1024]{2,1,0:T(8,128)(2,1)S(1)}, u32[]{:S(2)}, u32[]{:S(2)}) collective-permute-start(bf16[2,128,1024]{2,1,0:T(8,128)(2,1)S(1)} %fusion.32), channel_id=1, source_target_pairs={{1,0},{2,1},{3,2},{4,3},{5,4},{6,5},{7,6},{0,7},{9,8},{10,9},{11,1... | collective-permute-start | bytes 1572872 | tf_op jit(solution)/shard_map/ppermute | solution.py:19
  16.6 20.3 %collective-permute-start = (bf16[2,128,1024]{2,1,0:T(8,128)(2,1)S(1)}, bf16[2,128,1024]{2,1,0:T(8,128)(2,1)S(1)}, u32[]{:S(2)}, u32[]{:S(2)}) collective-permute-start(bf16[2,128,1024]{2,1,0:T(8,128)(2,1)S(1)} %fusion.32), channel_id=1, source_target_pairs={{0,1},{1,2},{2,3},{3,4},{4,5},{5,6},{6,7},{7,0},{8,9},{9,10},{10,1... | collective-permute-start | bytes 1572872 | tf_op jit(solution)/shard_map/ppermute | solution.py:16
  36.8 9.2 %copy-start.9 = (f32[1024]{0:T(1024)S(1)}, f32[1024]{0:T(1024)}, u32[]{:S(2)}) copy-start(f32[1024]{0:T(1024)} %param.10) | copy-start | bytes 12292
  46.1 19.5 %copy-start.2 = (f32[100,2048]{1,0:T(8,128)S(1)}, f32[100,2048]{1,0:T(8,128)}, u32[]{:S(2)}) copy-start(f32[100,2048]{1,0:T(8,128)} %param.14) | copy-start | bytes 2457604
  46.1 19.5 %copy-start.5 = (bf16[100,1024]{1,0:T(8,128)(2,1)S(1)}, bf16[100,1024]{1,0:T(8,128)(2,1)}, u32[]{:S(2)}) copy-start(bf16[100,1024]{1,0:T(8,128)(2,1)} %param.11) | copy-start | bytes 614404
  130.9 5.3 %copy-start.8 = (f32[2048]{0:T(1024)S(1)}, f32[2048]{0:T(1024)}, u32[]{:S(2)}) copy-start(f32[2048]{0:T(1024)} %param.15) | copy-start | bytes 24580
  132.6 25.0 %all-to-all-start.1 = ((f32[8,100,512]{2,1,0:T(8,128)}), f32[8,100,512]{2,1,0:T(8,128)S(1)}, u32[]{:S(2)}, u32[]{:S(2)}) async-start(f32[8,100,512]{2,1,0:T(8,128)} %multiply_subtract_fusion), calls=%async_computation.1 | async-start | bytes 3407872 | tf_op jit(solution)/shard_map/all_to_all | solution.py:76
  136.2 176.8 %reduce-scatter.2.cloned.1.call-start = ((), (), s32[]{:S(2)}) async-start(), calls=%async_computation.4 | async-start | bytes 4718592 | tf_op jit(solution)/shard_map/reduce_scatter | solution.py:103
  162.4 20.3 %copy-start.3 = (f32[2,100,2048]{2,1,0:T(8,128)}, f32[2,100,2048]{2,1,0:T(8,128)S(1)}, u32[]{:S(2)}) copy-start(f32[2,100,2048]{2,1,0:T(8,128)S(1)} %all_to_all.33) | copy-start | bytes 4915204
  182.7 8.4 %copy-start.10 = (bf16[2,2048,1024]{1,2,0:T(8,128)(2,1)S(1)}, bf16[2,2048,1024]{1,2,0:T(8,128)(2,1)}, u32[]{:S(2)}) copy-start(bf16[2,2048,1024]{1,2,0:T(8,128)(2,1)} %get-tuple-element.37) | copy-start | bytes 25165828
  191.1 10.2 %copy-start.4 = (bf16[2,128,1024]{2,1,0:T(8,128)(2,1)S(1)}, bf16[2,128,1024]{2,1,0:T(8,128)(2,1)}, u32[]{:S(2)}) copy-start(bf16[2,128,1024]{2,1,0:T(8,128)(2,1)} %param.8) | copy-start | bytes 1572868
  196.3 25.5 %collective-permute-start.2 = (bf16[2,128,1024]{1,2,0:T(8,128)(2,1)S(1)}, bf16[2,128,1024]{1,2,0:T(8,128)(2,1)S(1)}, u32[]{:S(2)}, u32[]{:S(2)}) collective-permute-start(bf16[2,128,1024]{1,2,0:T(8,128)(2,1)S(1)} %get-tuple-element.27), channel_id=1, source_target_pairs={{0,7},{1,0},{2,1},{3,2},{4,3},{5,4},{6,5},{7,6},{8,15},{9,8},{10,9... | collective-permute-start | bytes 1572872 | tf_op jit(solution)/shard_map/ppermute | solution.py:27
  201.3 21.3 %collective-permute-start.3 = (bf16[2,128,1024]{1,2,0:T(8,128)(2,1)S(1)}, bf16[2,128,1024]{1,2,0:T(8,128)(2,1)S(1)}, u32[]{:S(2)}, u32[]{:S(2)}) collective-permute-start(bf16[2,128,1024]{1,2,0:T(8,128)(2,1)S(1)} %get-tuple-element.26), channel_id=1, source_target_pairs={{0,1},{1,2},{2,3},{3,4},{4,5},{5,6},{6,7},{7,0},{8,9},{9,10},{10,1... | collective-permute-start | bytes 1572872 | tf_op jit(solution)/shard_map/ppermute | solution.py:27
  225.2 126.4 %all-reduce.7.cloned.1.call-start = ((), (), s32[]{:S(2)}) async-start(), calls=%async_computation.5 | async-start | bytes 1900544 | tf_op jit(solution)/shard_map/psum | solution.py:102
  225.5 203.3 %copy-start.1 = (bf16[1024,1024]{1,0:T(8,128)(2,1)S(1)}, bf16[1024,1024]{1,0:T(8,128)(2,1)}, u32[]{:S(2)}) copy-start(bf16[1024,1024]{1,0:T(8,128)(2,1)} %param.9) | copy-start | bytes 6291460
  313.0 114.0 %all-reduce.5.cloned.1.call-start = ((), (), s32[]{:S(2)}) async-start(), calls=%async_computation.3 | async-start | bytes 851968 | tf_op jit(solution)/shard_map/psum | solution.py:89
Sparse Core Ops, SparseCore 0:
  225.4 87.5 reduce-scatter.1
  316.3 35.3 all-reduce.6
  355.1 71.9 all-reduce.4
where the time goes:
time: 446 us; the launch traced here: 437 us
  waiting for transfers between devices  219 us (49%)
  matrix products  80.6 us (18%)
  blocking collectives  58 us (13%)
  other arithmetic  29 us (7%)
  local copies, waits for them, and re-layouts  18.2 us (4%)
  between operations  16.6 us (4%)
  starting transfers between devices  14.9 us (3%)
    reduce_scatter x1, waiting for transfers between devices, local(): lax.psum_scatter(summed, 'region', scatter_dimension=0, tiled=True)  80 us
    psum x1, waiting for transfers between devices, local(): region_heads = lax.psum((head[1], head[2]), 'region')  39.5 us
    psum x1, waiting for transfers between devices, local(): summed = lax.psum(total, 'member')  38.6 us
    all_to_all x1, blocking collectives, local(): lax.all_to_all(errors, 'member', split_axis=2, concat_axis=0, tiled=True)  29.6 us
    reduce_sum x1, other arithmetic, local(): pair_total = jnp.sum(dist, axis=(0, 1)) - count * smooth_width  23.3 us
    psum x1, blocking collectives, local(): region_heads = lax.psum((head[1], head[2]), 'region')  22.1 us
    all_to_all x1, waiting for transfers between devices, local(): lax.all_to_all(bracket_here, 'member', split_axis=0, concat_axis=2, tiled...  21.4 us
    dot_general x1, matrix products, local(): jnp.einsum('mvg,vh->mgh', dpred, w_out, preferred_element_type=jnp.float32)  20.2 us
  transfers between devices with their start and end apart: 8, of which 7 were waited for; matrix products, arithmetic and copies ran while one was open for 3% of the time, Pallas kernels for 0%

commit v1 on v0

v1 whole, which is shorter than its diff:
```python
import functools

import jax
import jax.numpy as jnp
from jax import lax
from jax.experimental import pallas as pl
from jax.experimental.pallas import tpu as pltpu
from jax.sharding import PartitionSpec as P

smooth_sq = 0.01
gelu_c = 0.7978845608028654
gelu_a = 0.044715
MESH = pl.DeviceIdType.MESH
BF = jnp.bfloat16
F32 = jnp.float32


def decoder(
    n_member, n_region, variables,
    latent, w_node, bias, w_out, src, weight, src_t, weight_t, target, area,
    grad_node, head_out, loss_out,
    ext, proj, adj, adj_t, hid, slope, preds, dpr, acc, gout, lacc, cb,
    part, recv_c, sum_c, recv_y, sum_y, recv_x, sum_x, recv_z, ob, lbuf,
    halo_s, halo_r, relay_s, relay_r, pa_s, pa_r, pb_s, pb_r, pf_s, pf_r,
    red_s, red_r, z_s, z_r, h_s, h_r, o_s, o_r, l_s, l_r,
):
    here, nodes, width = latent.shape
    points, fanout = src.shape
    span = 3 * nodes
    vp = w_out.shape[0]
    chunks, wide, gc = adj_t.shape
    rb = width // n_region
    quarter = width // 4
    half_n = n_region // 2
    count = here * n_member
    m = lax.axis_index("member")
    r = lax.axis_index("region")
    core = m % 2
    yy = m // 2
    xx = r % 2
    zz = r // 2
    m_core = m + 1 - 2 * core
    m_y = (1 - yy) * 2 + core
    m_diag = (1 - yy) * 2 + 1 - core
    r_x = r + 1 - 2 * xx
    r_relay = (r + n_region + 2 - 4 * xx) % n_region

    def remote(a, b, s, t, mm, rr):
        return pltpu.make_async_remote_copy(
            src_ref=a, dst_ref=b, send_sem=s, recv_sem=t, device_id=(mm, rr), device_id_type=MESH
        )

    barrier = pltpu.get_barrier_semaphore()
    for mm in (m_core, m_y, m_diag):
        pl.semaphore_signal(barrier, inc=1, device_id=(mm, r), device_id_type=MESH)
    for k in range(1, n_region):
        pl.semaphore_signal(
            barrier, inc=1, device_id=(m, (r + k) % n_region), device_id_type=MESH
        )
    pl.semaphore_wait(barrier, n_region + 2)

    far = 2 * xx
    near = 2 - far
    pieces = [(a, b) for a in range(here) for b in range(2)]
    hn = nodes // 2

    def halo(i):
        a, b = pieces[i]
        rows = pl.ds(b * hn, hn)
        return remote(
            latent.at[a, rows], ext.at[far, a, rows], halo_s.at[i], halo_r.at[i], m, r_x
        )

    def relay(i):
        a, b = pieces[i]
        rows = pl.ds(b * hn, hn)
        return remote(
            ext.at[near, a, rows], ext.at[far, a, rows], relay_s.at[i], relay_r.at[i], m, r_relay
        )

    for i in range(len(pieces)):
        halo(i).start()

    def project(slot, x):
        y = jnp.dot(
            x.reshape(here * nodes, width), w_node[...], preferred_element_type=F32
        ).astype(BF)
        for a in range(here):
            proj[a, pl.ds(pl.multiple_of(slot * nodes, nodes), nodes), :] = y[
                a * nodes : (a + 1) * nodes
            ]

    ext[1] = latent[...]
    project(1, latent[...])

    per = chunks // len(pieces)

    def build(c, _):
        rows = pl.ds(pl.multiple_of(c * gc, gc), gc)
        lane = lax.broadcasted_iota(jnp.int32, (gc, span), 1)
        row = lax.broadcasted_iota(jnp.int32, (span, gc), 0)
        s = src[rows, :]
        w = weight[rows, :]
        st = src_t[:, rows]
        wt = weight_t[:, rows]
        a = jnp.zeros((gc, span), F32)
        at = jnp.zeros((span, gc), F32)
        for k in range(fanout):
            a = a + jnp.where(s[:, k : k + 1] == lane, w[:, k : k + 1], 0.0)
            at = at + jnp.where(st[k : k + 1, :] == row, wt[k : k + 1, :], 0.0)
        adj[rows, :] = a.astype(BF)
        adj_t[c, 0:span, :] = at.astype(BF)
        adj_t[c, span:wide, :] = jnp.ones((wide - span, gc), BF)
        return 0

    for i in range(len(pieces)):
        lax.fori_loop(i * per, (i + 1) * per, build, 0)
        halo(i).wait_recv()
        relay(i).start()
    project(near, ext[near])
    for i in range(len(pieces)):
        relay(i).wait_recv()
    project(far, ext[far])

    lag = chunks // 2

    def to_core(c):
        return remote(preds.at[0, c], preds.at[1, c], pa_s.at[c], pa_r.at[c], m_core, r)

    def to_y(c):
        return remote(preds.at[0, c], preds.at[2, c], pb_s.at[c], pb_r.at[c], m_y, r)

    def pass_on(c):
        return remote(preds.at[2, c], preds.at[3, c], pf_s.at[c], pf_r.at[c], m_core, r)

    def forward(c, _):
        rows = pl.ds(pl.multiple_of(c * gc, gc), gc)
        for a in range(here):
            x = jnp.dot(adj[rows, :], proj[a], preferred_element_type=F32) + bias[...]
            u = x * x
            t = jnp.tanh(x * (gelu_c + gelu_c * gelu_a * u))
            p = 0.5 + 0.5 * t
            h = x * p
            hb = h.astype(BF)
            hid[a, rows, :] = hb
            sl = p + h * (1.0 - p) * (2.0 * gelu_c + 6.0 * gelu_c * gelu_a * u)
            slope[a, rows, :] = sl.astype(BF)
            preds[0, c, a] = lax.dot_general(
                w_out[...], hb, (((1,), (1,)), ((), ())), preferred_element_type=F32
            ).astype(BF)
        to_core(c).start()
        to_y(c).start()

        @pl.when(c >= lag)
        def _():
            to_y(c - lag).wait_recv()
            pass_on(c - lag).start()

        return 0

    lax.fori_loop(0, chunks, forward, 0)

    acc[...] = jnp.zeros_like(acc)
    gout[...] = jnp.zeros_like(gout)
    lacc[...] = jnp.zeros_like(lacc)
    step = 16

    def backward(c, _):
        rows = pl.ds(pl.multiple_of(c * gc, gc), gc)

        @pl.when(c < chunks - lag)
        def _():
            to_y(c + lag).wait_recv()
            pass_on(c + lag).start()

        to_core(c).wait_recv()
        pass_on(c).wait_recv()
        arow = area[:, rows]
        ascale = arow * (1.0 / variables)
        for v in range(0, vp, step):
            vs = slice(v, v + step)
            ps = [preds[s, c, a, vs, :].astype(F32) for s in range(4) for a in range(here)]
            tg = target[vs, rows]
            dist = jnp.zeros((step, gc), F32)
            sums = [jnp.zeros((step, gc), F32) for _ in range(here)]
            for a in range(here):
                for b in range(a + 1, count):
                    d = ps[a] - ps[b]
                    q = d * d + smooth_sq
                    i = lax.rsqrt(q)
                    g = d * i
                    sums[a] = sums[a] + g
                    s = q * i
                    if b < here:
                        sums[b] = sums[b] - g
                        s = s + s
                    dist = dist + s
            total = dist * (-1.0 / (2.0 * count * (count - 1)))
            for a in range(here):
                e = ps[a] - tg
                q = e * e + smooth_sq
                i = lax.rsqrt(q)
                total = total + q * i * (1.0 / count)
                br = e * i * (1.0 / count) - sums[a] * (1.0 / (count * (count - 1)))
                dpr[a, vs, :] = (br * ascale).astype(BF)
            total = total * arow
            if v + step > variables:
                keep = lax.broadcasted_iota(jnp.int32, (step, gc), 0) < variables - v
                total = jnp.where(keep, total, 0.0)
            lacc[...] += total
        for a in range(here):
            dp = dpr[a]
            hb = hid[a, rows, :]
            gout[0:vp] += jnp.dot(dp, hb, preferred_element_type=F32)
            dh = lax.dot_general(
                dp, w_out[...], (((0,), (0,)), ((), ())), preferred_element_type=F32
            )
            dpre = (dh * slope[a, rows, :].astype(F32)).astype(BF)
            acc[a] += jnp.dot(adj_t[c], dpre, preferred_element_type=F32)
        return 0

    lax.fori_loop(0, chunks, backward, 0)

    lbuf[0] = jnp.broadcast_to(
        jnp.sum(lacc[...]) * (1.0 / (variables * points)), lbuf.shape[1:]
    )

    def share_loss(k, mm):
        return remote(lbuf.at[0], lbuf.at[k], l_s.at[k - 1], l_r.at[k - 1], mm, r)

    sharing = [share_loss(k + 1, mm) for k, mm in enumerate((m_core, m_y, m_diag))]
    for copy in sharing:
        copy.start()

    bias_row = acc[0, span : span + 1, :]
    for a in range(1, here):
        bias_row = bias_row + acc[a, span : span + 1, :]
    gout[vp : vp + 1] = bias_row
    for a in range(here):
        for s in range(3):
            cb[s, a] = acc[a, s * nodes : (s + 1) * nodes, :].astype(BF)

    tall = 256
    for i in range(0, width, tall):
        left = ext[:, :, :, i : i + tall].reshape(span * here, tall)
        g = lax.dot_general(
            left, cb[...].reshape(span * here, width), (((0,), (0,)), ((), ())),
            preferred_element_type=F32,
        ).astype(BF)
        for j in range(tall // rb):
            q = i // rb + j
            for k in range(4):
                part[k // 2, k % 2, q % 2, q // 2, 0:rb, :] = g[
                    j * rb : (j + 1) * rb, k * quarter : (k + 1) * quarter
                ]
    for q in range(n_region):
        hv = gout[16 * q : 16 * q + 16, :].astype(BF)
        for k in range(4):
            part[k // 2, k % 2, q % 2, q // 2, rb : rb + 16, :] = hv[
                :, k * quarter : (k + 1) * quarter
            ]

    def add(a, b):
        return a.astype(F32) + b.astype(F32)

    c_copy = remote(part.at[1 - core], recv_c, red_s.at[0], red_r.at[0], m_core, r)
    c_copy.start()
    c_copy.wait_recv()

    def add_c(i, _):
        for k in range(2):
            for j in range(2):
                sum_c[k, j, i] = add(part[core, k, j, i], recv_c[k, j, i]).astype(BF)
        return 0

    lax.fori_loop(0, half_n, add_c, 0)
    y_copy = remote(sum_c.at[1 - yy], recv_y, red_s.at[1], red_r.at[1], m_y, r)
    y_copy.start()
    y_copy.wait_recv()

    def add_y(i, _):
        for j in range(2):
            sum_y[j, i] = add(sum_c[yy, j, i], recv_y[j, i]).astype(BF)
        return 0

    lax.fori_loop(0, half_n, add_y, 0)
    x_copy = remote(sum_y.at[1 - xx], recv_x, red_s.at[2], red_r.at[2], m, r_x)
    x_copy.start()
    x_copy.wait_recv()

    def add_x(i, _):
        sum_x[i] = add(sum_y[xx, i], recv_x[i]).astype(BF)
        return 0

    lax.fori_loop(0, half_n, add_x, 0)
    z_copies = []
    for k in range(1, half_n):
        z_to = (zz + k) % half_n
        z_copies.append(
            remote(
                sum_x.at[z_to], recv_z.at[k - 1], z_s.at[k - 1], z_r.at[k - 1], m, 2 * z_to + xx
            )
        )
    for copy in z_copies:
        copy.start()
    total = sum_x[zz].astype(F32)
    for k in range(1, half_n):
        z_copies[k - 1].wait_recv()
        total = total + recv_z[k - 1].astype(F32)
    ob[0, 0:rb, :] = total[0:rb]
    mine = pl.ds(pl.multiple_of(rb + 16 * r, 16), 16)
    ob[0, mine, :] = total[rb : rb + 16]
    h_copies = [
        remote(
            ob.at[0, mine], ob.at[0, mine], h_s.at[k - 1], h_r.at[k - 1], m, (r + k) % n_region
        )
        for k in range(1, n_region)
    ]
    for copy in h_copies:
        copy.start()
    for copy in h_copies:
        copy.wait_recv()
    o_core = remote(ob.at[0], ob.at[1], o_s.at[0], o_r.at[0], m_core, r)
    o_y = remote(ob.at[0], ob.at[2], o_s.at[1], o_r.at[1], m_y, r)
    o_pass = remote(ob.at[2], ob.at[3], o_s.at[2], o_r.at[2], m_core, r)
    o_y.start()
    o_core.start()

    def place(k, mm):
        at = pl.ds(pl.multiple_of(((mm % 2) * 2 + mm // 2) * quarter, quarter), quarter)
        grad_node[:, at] = ob[k, 0:rb, :]
        head_out[:, at] = ob[k, rb:, :]

    place(0, m)
    lsum = lbuf[0]
    for k, copy in enumerate(sharing):
        copy.wait_recv()
        lsum = lsum + lbuf[k + 1]
    loss_out[...] = lsum
    o_core.wait_recv()
    place(1, m_core)
    o_y.wait_recv()
    o_pass.start()
    place(2, m_y)
    o_pass.wait_recv()
    place(3, m_diag)

    for i in range(len(pieces)):
        halo(i).wait_send()
        relay(i).wait_send()

    def drain(c, _):
        to_core(c).wait_send()
        to_y(c).wait_send()
        pass_on(c).wait_send()
        return 0

    lax.fori_loop(0, chunks, drain, 0)
    for copy in [c_copy, y_copy, x_copy, o_core, o_y, o_pass] + z_copies + h_copies + sharing:
        copy.wait_send()


def local(n_member, n_region, latent, w_node, bias, w_out, edge_src, edge_weight, target, area):
    here, nodes, width = latent.shape
    points, fanout = edge_src.shape
    variables = target.shape[0]
    vp = -(-variables // 16) * 16
    gc = 256
    chunks = points // gc
    span = 3 * nodes
    wide = span + 16
    rb = width // n_region
    head = 16 * n_region
    quarter = width // 4
    half_n = n_region // 2
    blk = rb + 16
    grow = max(head, vp + 16)
    dma = lambda k: pltpu.SemaphoreType.DMA((k,))
    vm = lambda shape, t: pltpu.VMEM(shape, t)
    grad_node, heads, loss = pl.pallas_call(
        functools.partial(decoder, n_member, n_region, variables),
        out_shape=(
            jax.ShapeDtypeStruct((rb, width), F32),
            jax.ShapeDtypeStruct((head, width), F32),
            jax.ShapeDtypeStruct((8, 128), F32),
        ),
        in_specs=[pl.BlockSpec(memory_space=pltpu.VMEM)] * 10,
        out_specs=[pl.BlockSpec(memory_space=pltpu.VMEM)] * 3,
        scratch_shapes=[
            vm((3, here, nodes, width), BF),
            vm((here, span, width), BF),
            vm((points, span), BF),
            vm((chunks, wide, gc), BF),
            vm((here, points, width), BF),
            vm((here, points, width), BF),
            vm((4, chunks, here, vp, gc), BF),
            vm((here, vp, gc), BF),
            vm((here, wide, width), F32),
            vm((grow, width), F32),
            vm((16, gc), F32),
            vm((3, here, nodes, width), BF),
            vm((2, 2, 2, half_n, blk, quarter), BF),
            vm((2, 2, half_n, blk, quarter), BF),
            vm((2, 2, half_n, blk, quarter), BF),
            vm((2, half_n, blk, quarter), BF),
            vm((2, half_n, blk, quarter), BF),
            vm((half_n, blk, quarter), BF),
            vm((half_n, blk, quarter), BF),
            vm((half_n - 1, blk, quarter), BF),
            vm((4, rb + head, quarter), F32),
            vm((4, 8, 128), F32),
            dma(4), dma(4), dma(4), dma(4),
            dma(chunks), dma(chunks), dma(chunks), dma(chunks), dma(chunks), dma(chunks),
            dma(3), dma(3), dma(half_n - 1), dma(half_n - 1),
            dma(n_region - 1), dma(n_region - 1), dma(3), dma(3), dma(3), dma(3),
        ],
        compiler_params=pltpu.CompilerParams(
            collective_id=0, has_side_effects=True, vmem_limit_bytes=60 * 2**20
        ),
    )(
        latent, w_node, bias.reshape(1, width),
        jnp.pad(w_out, ((0, vp - variables), (0, 0))),
        edge_src, edge_weight, edge_src.T, edge_weight.T,
        jnp.pad(target, ((0, vp - variables), (0, 0))), area.reshape(1, points),
    )
    return (grad_node, heads[:variables], heads[vp], loss[0, 0:1])


def solution(mesh):
    return jax.shard_map(
        functools.partial(local, mesh.shape["member"], mesh.shape["region"]),
        mesh=mesh,
        in_specs=(
            P("member", "region", None),
            P(),
            P(),
            P(),
            P("region", None),
            P("region", None),
            P(None, "region"),
            P("region"),
        ),
        out_specs=(P("region", None), P(), P(), P("region")),
        check_vma=False,
    )
```

time: 446 us -> 119 us (0.27); the launches traced: 437 us -> 118 us
  waiting for transfers between devices: 219 us -> 0 us
  Pallas kernels: 0 us -> 105 us
  matrix products: 80.6 us -> 0 us
  blocking collectives: 58 us -> 0 us
  other arithmetic: 29 us -> 0 us
  between operations: 16.6 us -> 0.66 us
  starting transfers between devices: 14.9 us -> 0 us
  local copies, waits for them, and re-layouts: 18.2 us -> 12.8 us
    pallas_call x0 -> x1, Pallas kernels: none -> 105 us  [local(): pl.pallas_call(functools.partial(decoder, n_member, n_region, variables),...]
    dot_general x11 -> x0, matrix products: 80.6 us -> none  [the longest x1 20.2 us: local(): jnp.einsum('mvg,vh->mgh', dpred, w_out, preferred_element_type=jnp.float32)]
    reduce_scatter x1 -> x0, waiting for transfers between devices: 80 us -> none  [local(): lax.psum_scatter(summed, 'region', scatter_dimension=0, tiled=True)]
    psum x2 -> x0, waiting for transfers between devices: 78 us -> none  [the longest x1 39.5 us: local(): region_heads = lax.psum((head[1], head[2]), 'region')]
    ppermute x4 -> x0, waiting for transfers between devices: 40.1 us -> none  [the longest x1 20.1 us: padded(): lax.ppermute(lax.slice_in_dim(block, 0, width, axis=dim), axis, backward)]
    all_to_all x1 -> x0, blocking collectives: 29.6 us -> none  [local(): lax.all_to_all(errors, 'member', split_axis=2, concat_axis=0, tiled=True)]
    psum x2 -> x0, blocking collectives: 28.4 us -> none  [the longest x1 22.1 us: local(): region_heads = lax.psum((head[1], head[2]), 'region')]
    reduce_sum x3 -> x0, other arithmetic: 27.3 us -> none  [the longest x1 23.3 us: local(): pair_total = jnp.sum(dist, axis=(0, 1)) - count * smooth_width]
  transfers between devices with their start and end apart: 8 -> 0, of which waited for: 7 -> 0; matrix products, arithmetic and copies ran while one was open for 3% -> 0% of each run, Pallas kernels for 0% -> 0%
where the time goes in v1:
time: 119 us; the launch traced here: 118 us
  Pallas kernels  105 us (88%)
  local copies, waits for them, and re-layouts  12.8 us (11%)
    pallas_call x1, Pallas kernels, local(): pl.pallas_call(functools.partial(decoder, n_member, n_region, variables),...  105 us
    unnamed x7, local copies, waits for them, and re-layouts  4.63 us
    slice x3, local copies, waits for them, and re-layouts, local(): return (grad_node, heads[:variables], heads[vp], loss[0, 0:1])  4.34 us

profile of v1, /device:TPU:0, one launch (start us, length us, event | category | flops | bytes accessed | tf_op | source)
XLA Modules:
  0.0 118.4 jit_solution(3152798696316557032)
XLA Ops:
  0.6 0.0 copy-start.1
  0.6 0.0 copy-start
  0.7 1.6 %pad.8.w_out = bf16[112,1024]{1,0:T(8,128)(2,1)} pad(bf16[100,1024]{1,0:T(8,128)(2,1)} %param.11, bf16[]{:T(256)} %constant.3.clone.1), padding=0_12x0_0 | pad | bytes 434178 | tf_op jit(solution)/shard_map/jit(_pad)/pad | solution.py:422
  2.3 2.2 %pad.9.target = f32[112,2048]{1,0:T(8,128)} pad(f32[100,2048]{1,0:T(8,128)} %param.14, f32[]{:T(128)} %constant.4.clone.1), padding=0_12x0_0 | pad | bytes 1736708 | tf_op jit(solution)/shard_map/jit(_pad)/pad | solution.py:424
  4.5 0.0 copy-done
  4.5 1.3 %copy.12.src = s32[2048,3]{1,0:T(8,128)} copy(s32[2048,3]{0,1:T(4,128)S(1)} %copy-done) | data formatting | bytes 49152 | tf_op args[4]
  5.8 0.0 copy-done.1
  5.8 1.4 %copy.13.weight = f32[2048,3]{1,0:T(8,128)} copy(f32[2048,3]{0,1:T(4,128)S(1)} %copy-done.1) | data formatting | bytes 49152 | tf_op args[5]
  7.2 105.0 %shard_map.111 = (f32[128,1024]{1,0:T(8,128)}, f32[128,1024]{1,0:T(8,128)}, f32[8,128]{1,0:T(8,128)}) custom-call(bf16[2,128,1024]{2,1,0:T(8,128)(2,1)} %latent.1, bf16[1024,1024]{1,0:T(8,128)(2,1)} %w_node.1, f32[1,1024]{1,0:T(1,128)} %bitcast.9, bf16[112,1024]{1,0:T(8,128)(2,1)} %pad.8.w_out, s32[2048,3]{1,0:T(8,128)} %copy.12.src, ...), custom_call_target="tpu_custom_call" | custom-call | tf_op jit(solution)/shard_map/pallas_call | solution.py:380
  112.2 1.2 %slice.11 = f32[1,1]{1,0:T(1,128)} slice(f32[8,128]{1,0:T(8,128)} %get-tuple-element.9), slice={[0:1], [0:1]} | slice | bytes 8 | tf_op jit(solution)/shard_map/slice | solution.py:426
  113.4 1.4 %slice.10 = f32[1,1024]{1,0:T(1,128)} slice(f32[128,1024]{1,0:T(8,128)} %get-tuple-element.8), slice={[112:113], [0:1024]} | slice | bytes 8192 | tf_op jit(solution)/shard_map/slice | solution.py:426
  114.7 1.8 %slice.9 = f32[100,1024]{1,0:T(8,128)} slice(f32[128,1024]{1,0:T(8,128)} %get-tuple-element.8), slice={[0:100], [0:1024]} | slice | bytes 819200 | tf_op jit(solution)/shard_map/slice | solution.py:426
  116.5 1.9 %copy.15 = f32[128,1024]{1,0:T(8,128)} copy(f32[128,1024]{1,0:T(8,128)} %get-tuple-element.14) | data formatting | bytes 1048576
Async XLA Ops:
  0.6 5.2 %copy-start.1 = (f32[2048,3]{0,1:T(4,128)S(1)}, f32[2048,3]{0,1:T(4,128)}, u32[]{:S(2)}) copy-start(f32[2048,3]{0,1:T(4,128)} %param.13) | copy-start | bytes 73732
  0.6 3.8 %copy-start = (s32[2048,3]{0,1:T(4,128)S(1)}, s32[2048,3]{0,1:T(4,128)}, u32[]{:S(2)}) copy-start(s32[2048,3]{0,1:T(4,128)} %param.12) | copy-start | bytes 73732

commit v2 on v1

v2 whole, which is shorter than its diff:
```python
import functools

import jax
import jax.numpy as jnp
from jax import lax
from jax.experimental import pallas as pl
from jax.experimental.pallas import tpu as pltpu
from jax.sharding import PartitionSpec as P

smooth_sq = 0.01
gelu_c = 0.7978845608028654
gelu_a = 0.044715
MESH = pl.DeviceIdType.MESH
BF = jnp.bfloat16
F32 = jnp.float32


def decoder(
    n_member, n_region, variables,
    latent, w_node, bias, w_out_in, src_t, weight_t, target, area,
    grad_node, grad_out, grad_bias, loss_out,
    w_out, tail, ext, proj, adj, adj_t, hid, slope, preds, dpr, acc, gout, lacc, cb,
    part, recv_c, sum_c, recv_1a, recv_1b, sum_1a, sum_1b, recv_2, sum_2, recv_z, ob, lbuf,
    halo_s, halo_r, relay_s, relay_r, pa_s, pa_r, pb_s, pb_r, pf_s, pf_r,
    c_s, c_r, red_s, red_r, z_s, z_r, h_s, h_r, o_s, o_r, l_s, l_r,
):
    here, nodes, width = latent.shape
    fanout, points = src_t.shape
    span = 3 * nodes
    vp = w_out.shape[0]
    chunks, wide, gc = adj_t.shape
    rb = width // n_region
    quarter = width // 4
    half_n = n_region // 2
    count = here * n_member
    m = lax.axis_index("member")
    r = lax.axis_index("region")
    core = m % 2
    yy = m // 2
    xx = r % 2
    zz = r // 2
    m_core = m + 1 - 2 * core
    m_y = (1 - yy) * 2 + core
    m_diag = (1 - yy) * 2 + 1 - core
    r_x = r + 1 - 2 * xx
    r_relay = (r + n_region + 2 - 4 * xx) % n_region

    def remote(a, b, s, t, mm, rr):
        return pltpu.make_async_remote_copy(
            src_ref=a, dst_ref=b, send_sem=s, recv_sem=t, device_id=(mm, rr), device_id_type=MESH
        )

    barrier = pltpu.get_barrier_semaphore()
    for mm in (m_core, m_y, m_diag):
        pl.semaphore_signal(barrier, inc=1, device_id=(mm, r), device_id_type=MESH)
    for k in range(1, n_region):
        pl.semaphore_signal(
            barrier, inc=1, device_id=(m, (r + k) % n_region), device_id_type=MESH
        )
    pl.semaphore_wait(barrier, n_region + 2)

    far = 2 * xx
    near = 2 - far
    pieces = [(a, b) for a in range(here) for b in range(2)]
    hn = nodes // 2

    def halo(i):
        a, b = pieces[i]
        rows = pl.ds(b * hn, hn)
        return remote(
            latent.at[a, rows], ext.at[far, a, rows], halo_s.at[i], halo_r.at[i], m, r_x
        )

    def relay(i):
        a, b = pieces[i]
        rows = pl.ds(b * hn, hn)
        return remote(
            ext.at[near, a, rows], ext.at[far, a, rows], relay_s.at[i], relay_r.at[i], m, r_relay
        )

    for i in range(len(pieces)):
        halo(i).start()

    def project(a):
        proj[a] = jnp.dot(
            ext[:, a].reshape(span, width), w_node[...], preferred_element_type=F32
        ).astype(BF)

    ext[1] = latent[...]
    w_out[0:variables] = w_out_in[...]
    w_out[variables:vp] = jnp.zeros((vp - variables, width), BF)
    tail[...] = jnp.zeros_like(tail)
    tail[0 : variables - (vp - 16)] = target[vp - 16 : variables]

    def build(c, _):
        rows = pl.ds(pl.multiple_of(c * gc, gc), gc)
        row = lax.broadcasted_iota(jnp.int32, (span, gc), 0)
        st = src_t[:, rows]
        wt = weight_t[:, rows]
        at = jnp.zeros((span, gc), F32)
        for k in range(fanout):
            at = at + jnp.where(st[k : k + 1, :] == row, wt[k : k + 1, :], 0.0)
        adj[rows, :] = at.T.astype(BF)
        adj_t[c, 0:span, :] = at.astype(BF)
        adj_t[c, span:wide, :] = jnp.ones((wide - span, gc), BF)
        return 0

    lax.fori_loop(0, chunks // 4, build, 0)
    halo(0).wait_recv()
    relay(0).start()
    lax.fori_loop(chunks // 4, chunks, build, 0)
    halo(1).wait_recv()
    relay(1).start()
    relay(0).wait_recv()
    relay(1).wait_recv()

    lag = chunks // 2

    def blocks(t):
        return t // chunks, t % chunks

    def to_core(t):
        a, c = blocks(t)
        return remote(preds.at[0, a, c], preds.at[1, a, c], pa_s.at[t], pa_r.at[t], m_core, r)

    def to_y(t):
        a, c = blocks(t)
        return remote(preds.at[0, a, c], preds.at[2, a, c], pb_s.at[t], pb_r.at[t], m_y, r)

    def pass_on(t):
        a, c = blocks(t)
        return remote(preds.at[2, a, c], preds.at[3, a, c], pf_s.at[t], pf_r.at[t], m_core, r)

    steps = here * chunks

    def forward(a, c):
        rows = pl.ds(pl.multiple_of(c * gc, gc), gc)
        t = a * chunks + c
        x = jnp.dot(adj[rows, :], proj[a], preferred_element_type=F32) + bias[...]
        u = x * x
        th = jnp.tanh(x * (gelu_c + gelu_c * gelu_a * u))
        p = 0.5 + 0.5 * th
        h = x * p
        hb = h.astype(BF)
        hid[a, rows, :] = hb
        sl = p + h * (1.0 - p) * (2.0 * gelu_c + 6.0 * gelu_c * gelu_a * u)
        slope[a, rows, :] = sl.astype(BF)
        preds[0, a, c] = lax.dot_general(
            w_out[...], hb, (((1,), (1,)), ((), ())), preferred_element_type=F32
        ).astype(BF)
        to_y(t).start()
        to_core(t).start()

        @pl.when(t >= lag)
        def _():
            to_y(t - lag).wait_recv()
            pass_on(t - lag).start()

    for a in range(here):
        project(a)

        def run(c, _):
            if a + 1 < here:
                for b in range(2):
                    @pl.when(c == 2 * b)
                    def _():
                        halo(2 * a + 2 + b).wait_recv()
                        relay(2 * a + 2 + b).start()

            forward(a, c)
            return 0

        lax.fori_loop(0, chunks, run, 0)
        if a + 1 < here:
            for b in range(2):
                relay(2 * a + 2 + b).wait_recv()

    acc[...] = jnp.zeros_like(acc)
    gout[...] = jnp.zeros_like(gout)
    lacc[...] = jnp.zeros_like(lacc)
    step = 16

    def backward(c, _):
        rows = pl.ds(pl.multiple_of(c * gc, gc), gc)

        @pl.when(c < lag)
        def _():
            to_y(steps - lag + c).wait_recv()
            pass_on(steps - lag + c).start()

        for a in range(here):
            to_core(a * chunks + c).wait_recv()
            pass_on(a * chunks + c).wait_recv()
        arow = area[:, rows]
        ascale = arow * (1.0 / variables)
        for v in range(0, vp, step):
            vs = slice(v, v + step)
            ps = [preds[s, a, c, vs, :].astype(F32) for s in range(4) for a in range(here)]
            tg = target[vs, rows] if v + step <= variables else tail[:, rows]
            dist = jnp.zeros((step, gc), F32)
            sums = [jnp.zeros((step, gc), F32) for _ in range(here)]
            for a in range(here):
                for b in range(a + 1, count):
                    d = ps[a] - ps[b]
                    q = d * d + smooth_sq
                    i = lax.rsqrt(q)
                    g = d * i
                    sums[a] = sums[a] + g
                    s = q * i
                    if b < here:
                        sums[b] = sums[b] - g
                        s = s + s
                    dist = dist + s
            total = dist * (-1.0 / (2.0 * count * (count - 1)))
            for a in range(here):
                e = ps[a] - tg
                q = e * e + smooth_sq
                i = lax.rsqrt(q)
                total = total + q * i * (1.0 / count)
                br = e * i * (1.0 / count) - sums[a] * (1.0 / (count * (count - 1)))
                dpr[a, vs, :] = (br * ascale).astype(BF)
            total = total * arow
            if v + step > variables:
                keep = lax.broadcasted_iota(jnp.int32, (step, gc), 0) < variables - v
                total = jnp.where(keep, total, 0.0)
            lacc[...] += total
        for a in range(here):
            dp = dpr[a]
            hb = hid[a, rows, :]
            gout[0:vp] += jnp.dot(dp, hb, preferred_element_type=F32)
            dh = lax.dot_general(
                dp, w_out[...], (((0,), (0,)), ((), ())), preferred_element_type=F32
            )
            dpre = (dh * slope[a, rows, :].astype(F32)).astype(BF)
            acc[a] += jnp.dot(adj_t[c], dpre, preferred_element_type=F32)
        return 0

    lax.fori_loop(0, chunks, backward, 0)

    lbuf[0] = jnp.broadcast_to(
        jnp.sum(lacc[...]) * (1.0 / (variables * points)), lbuf.shape[1:]
    )

    def share_loss(k, mm):
        return remote(lbuf.at[0], lbuf.at[k], l_s.at[k - 1], l_r.at[k - 1], mm, r)

    sharing = [share_loss(k + 1, mm) for k, mm in enumerate((m_core, m_y, m_diag))]
    for copy in sharing:
        copy.start()

    bias_row = acc[0, span : span + 1, :]
    for a in range(1, here):
        bias_row = bias_row + acc[a, span : span + 1, :]
    gout[vp : vp + 1] = bias_row
    for a in range(here):
        for s in range(3):
            cb[s * here + a] = acc[a, s * nodes : (s + 1) * nodes, :].astype(BF)

    def add(a, b):
        return a.astype(F32) + b.astype(F32)

    c_copies = [
        remote(part.at[0, k], recv_c.at[k], c_s.at[k], c_r.at[k], m_core, r) for k in range(2)
    ]
    tall = 256
    lanes = quarter // 2
    for hh, side in enumerate((1 - core, core)):
        cols = pl.ds(pl.multiple_of(side * 2 * quarter, 2 * quarter), 2 * quarter)
        right = cb[:, :, cols].reshape(span * here, 2 * quarter)
        for i in range(0, width, tall):
            left = ext[:, :, :, i : i + tall].reshape(span * here, tall)
            g = lax.dot_general(
                left, right, (((0,), (0,)), ((), ())), preferred_element_type=F32
            ).astype(BF)
            for j in range(tall // rb):
                q = i // rb + j
                for k in range(4):
                    part[hh, k % 2, k // 2, q % 2, q // 2, 0:rb, :] = g[
                        j * rb : (j + 1) * rb, k * lanes : (k + 1) * lanes
                    ]
        for q in range(n_region):
            hv = gout[16 * q : 16 * q + 16, cols].astype(BF)
            for k in range(4):
                part[hh, k % 2, k // 2, q % 2, q // 2, rb : rb + 16, :] = hv[
                    :, k * lanes : (k + 1) * lanes
                ]
        if hh == 0:
            for copy in c_copies:
                copy.start()

    def add_c(k):
        def body(i, _):
            for a in range(2):
                for b in range(2):
                    sum_c[k, a, b, i] = add(part[1, k, a, b, i], recv_c[k, a, b, i]).astype(BF)
            return 0

        lax.fori_loop(0, half_n, body, 0)

    a1 = remote(sum_c.at[0, 1 - yy], recv_1a, red_s.at[0], red_r.at[0], m_y, r)
    b1 = remote(sum_c.at[1, :, 1 - xx], recv_1b, red_s.at[1], red_r.at[1], m, r_x)
    a2 = remote(sum_1a.at[1 - xx], recv_2.at[0], red_s.at[2], red_r.at[2], m, r_x)
    b2 = remote(sum_1b.at[1 - yy], recv_2.at[1], red_s.at[3], red_r.at[3], m_y, r)
    for k, copy in enumerate((a1, b1)):
        c_copies[k].wait_recv()
        add_c(k)
        copy.start()

    def add_1a(i, _):
        for b in range(2):
            sum_1a[b, i] = add(sum_c[0, yy, b, i], recv_1a[b, i]).astype(BF)
        return 0

    def add_1b(i, _):
        for b in range(2):
            sum_1b[b, i] = add(sum_c[1, b, xx, i], recv_1b[b, i]).astype(BF)
        return 0

    a1.wait_recv()
    lax.fori_loop(0, half_n, add_1a, 0)
    a2.start()
    b1.wait_recv()
    lax.fori_loop(0, half_n, add_1b, 0)
    b2.start()

    def add_2a(i, _):
        sum_2[i, 0] = add(sum_1a[xx, i], recv_2[0, i]).astype(BF)
        return 0

    def add_2b(i, _):
        sum_2[i, 1] = add(sum_1b[yy, i], recv_2[1, i]).astype(BF)
        return 0

    a2.wait_recv()
    lax.fori_loop(0, half_n, add_2a, 0)
    b2.wait_recv()
    lax.fori_loop(0, half_n, add_2b, 0)
    z_copies = []
    for k in range(1, half_n):
        z_to = (zz + k) % half_n
        z_copies.append(
            remote(
                sum_2.at[z_to], recv_z.at[k - 1], z_s.at[k - 1], z_r.at[k - 1], m, 2 * z_to + xx
            )
        )
    for copy in z_copies:
        copy.start()
    mine = pl.ds(pl.multiple_of(rb + 16 * r, 16), 16)
    totals = [sum_2[zz, k].astype(F32) for k in range(2)]
    for i in range(1, half_n):
        z_copies[i - 1].wait_recv()
        for k in range(2):
            totals[k] = totals[k] + recv_z[i - 1, k].astype(F32)
    for k in range(2):
        at = slice(k * lanes, (k + 1) * lanes)
        ob[0, 0:rb, at] = totals[k][0:rb].astype(BF)
        ob[0, mine, at] = totals[k][rb : rb + 16].astype(BF)
    h_copies = [
        remote(
            ob.at[0, mine], ob.at[0, mine], h_s.at[k - 1], h_r.at[k - 1], m, (r + k) % n_region
        )
        for k in range(1, n_region)
    ]
    for copy in h_copies:
        copy.start()
    tops, lows = pl.ds(0, rb), pl.ds(rb, 16 * n_region)

    def spread(rows, k):
        one = remote(ob.at[0, rows], ob.at[1, rows], o_s.at[k], o_r.at[k], m_core, r)
        two = remote(ob.at[0, rows], ob.at[2, rows], o_s.at[k + 1], o_r.at[k + 1], m_y, r)
        on = remote(ob.at[2, rows], ob.at[3, rows], o_s.at[k + 2], o_r.at[k + 2], m_core, r)
        return one, two, on

    t_core, t_y, t_on = spread(tops, 0)
    b_core, b_y, b_on = spread(lows, 3)
    t_y.start()
    t_core.start()

    def columns(mm):
        return pl.ds(pl.multiple_of(((mm % 2) * 2 + mm // 2) * quarter, quarter), quarter)

    def place_top(k, mm):
        grad_node[:, columns(mm)] = ob[k, 0:rb, :].astype(F32)

    def place_low(k, mm):
        grad_out[:, columns(mm)] = ob[k, rb : rb + vp, :].astype(F32)[0:variables]
        grad_bias[:, columns(mm)] = ob[k, rb + vp : rb + vp + 16, :].astype(F32)[0:1]

    place_top(0, m)
    for copy in sharing:
        copy.wait_recv()
    loss_out[0] = jnp.max((lbuf[0] + lbuf[1]) + (lbuf[2] + lbuf[3]))
    for copy in h_copies:
        copy.wait_recv()
    b_y.start()
    b_core.start()
    t_y.wait_recv()
    t_on.start()
    place_top(2, m_y)
    t_core.wait_recv()
    place_top(1, m_core)
    place_low(0, m)
    b_y.wait_recv()
    b_on.start()
    place_low(2, m_y)
    b_core.wait_recv()
    place_low(1, m_core)
    t_on.wait_recv()
    place_top(3, m_diag)
    b_on.wait_recv()
    place_low(3, m_diag)

    for i in range(len(pieces)):
        halo(i).wait_send()
        relay(i).wait_send()

    def drain(c, _):
        to_core(c).wait_send()
        to_y(c).wait_send()
        pass_on(c).wait_send()
        return 0

    lax.fori_loop(0, steps, drain, 0)
    ends = [a1, b1, a2, b2, t_core, t_y, t_on, b_core, b_y, b_on]
    for copy in ends + c_copies + z_copies + h_copies + sharing:
        copy.wait_send()


def local(n_member, n_region, latent, w_node, bias, w_out, edge_src, edge_weight, target, area):
    here, nodes, width = latent.shape
    points, fanout = edge_src.shape
    variables = target.shape[0]
    vp = -(-variables // 16) * 16
    gc = 256
    chunks = points // gc
    span = 3 * nodes
    wide = span + 16
    rb = width // n_region
    head = 16 * n_region
    quarter = width // 4
    lanes = quarter // 2
    half_n = n_region // 2
    blk = rb + 16
    grow = max(head, vp + 16)
    dma = lambda k: pltpu.SemaphoreType.DMA((k,))
    vm = lambda shape, t: pltpu.VMEM(shape, t)
    grad_node, grad_out, grad_bias, loss = pl.pallas_call(
        functools.partial(decoder, n_member, n_region, variables),
        out_shape=(
            jax.ShapeDtypeStruct((rb, width), F32),
            jax.ShapeDtypeStruct((variables, width), F32),
            jax.ShapeDtypeStruct((1, width), F32),
            jax.ShapeDtypeStruct((1,), F32),
        ),
        in_specs=[pl.BlockSpec(memory_space=pltpu.VMEM)] * 8,
        out_specs=[pl.BlockSpec(memory_space=pltpu.VMEM)] * 3
        + [pl.BlockSpec(memory_space=pltpu.SMEM)],
        scratch_shapes=[
            vm((vp, width), BF),
            vm((16, points), F32),
            vm((3, here, nodes, width), BF),
            vm((here, span, width), BF),
            vm((points, span), BF),
            vm((chunks, wide, gc), BF),
            vm((here, points, width), BF),
            vm((here, points, width), BF),
            vm((4, here, chunks, vp, gc), BF),
            vm((here, vp, gc), BF),
            vm((here, wide, width), F32),
            vm((grow, width), F32),
            vm((16, gc), F32),
            vm((3 * here, nodes, width), BF),
            vm((2, 2, 2, 2, half_n, blk, lanes), BF),
            vm((2, 2, 2, half_n, blk, lanes), BF),
            vm((2, 2, 2, half_n, blk, lanes), BF),
            vm((2, half_n, blk, lanes), BF),
            vm((2, half_n, blk, lanes), BF),
            vm((2, half_n, blk, lanes), BF),
            vm((2, half_n, blk, lanes), BF),
            vm((2, half_n, blk, lanes), BF),
            vm((half_n, 2, blk, lanes), BF),
            vm((half_n - 1, 2, blk, lanes), BF),
            vm((4, rb + head, quarter), BF),
            vm((4, 8, 128), F32),
            dma(4), dma(4), dma(4), dma(4),
            *[dma(here * chunks) for _ in range(6)],
            dma(2), dma(2), dma(4), dma(4), dma(half_n - 1), dma(half_n - 1),
            dma(n_region - 1), dma(n_region - 1), dma(6), dma(6), dma(3), dma(3),
        ],
        compiler_params=pltpu.CompilerParams(
            collective_id=0, has_side_effects=True, vmem_limit_bytes=60 * 2**20
        ),
    )(
        latent, w_node, bias.reshape(1, width), w_out, edge_src.T, edge_weight.T, target,
        area.reshape(1, points),
    )
    return (grad_node, grad_out, grad_bias.reshape(width), loss)


def solution(mesh):
    return jax.shard_map(
        functools.partial(local, mesh.shape["member"], mesh.shape["region"]),
        mesh=mesh,
        in_specs=(
            P("member", "region", None),
            P(),
            P(),
            P(),
            P("region", None),
            P("region", None),
            P(None, "region"),
            P("region"),
        ),
        out_specs=(P("region", None), P(), P(), P("region")),
        check_vma=False,
    )
```

time: 119 us -> 97.9 us (0.82)
  Pallas kernels: 105 us -> 90.2 us
  local copies, waits for them, and re-layouts: 12.8 us -> 4.94 us
  between operations: 0.66 us -> 2.45 us
    pallas_call x1, Pallas kernels: 105 us -> 90.2 us  [local(): pl.pallas_call(functools.partial(decoder, n_member, n_region, variables),...]
    slice x3 -> x0, local copies, waits for them, and re-layouts: 4.34 us -> none  [local(): return (grad_node, heads[:variables], heads[vp], loss[0, 0:1])]
    pad x2 -> x0, local copies, waits for them, and re-layouts: 3.81 us -> none  [the longest x1 2.16 us: local(): jnp.pad(target, ((0, vp - variables), (0, 0)))]
    unnamed x7 -> x3, local copies, waits for them, and re-layouts: 4.63 us -> 4.94 us
where the time goes in v2:
time: 97.9 us; the launch traced here: 97.6 us
  Pallas kernels  90.2 us (92%)
  local copies, waits for them, and re-layouts  4.94 us (5%)
  between operations  2.45 us (3%)
    pallas_call x1, Pallas kernels, local(): pl.pallas_call(functools.partial(decoder, n_member, n_region, variables),...  90.2 us
    unnamed x3, local copies, waits for them, and re-layouts  4.94 us

profile of v2, /device:TPU:0, one launch (start us, length us, event | category | flops | bytes accessed | tf_op | source)
XLA Modules:
  0.0 97.6 jit_solution(8140608285999724810)
XLA Ops:
  0.6 90.2 %shard_map.111 = (f32[128,1024]{1,0:T(8,128)}, f32[100,1024]{1,0:T(8,128)}, f32[1,1024]{1,0:T(1,128)}, f32[1]{0:T(128)}) custom-call(bf16[2,128,1024]{2,1,0:T(8,128)(2,1)} %latent.1, bf16[1024,1024]{1,0:T(8,128)(2,1)} %w_node.1, f32[1,1024]{1,0:T(1,128)} %bitcast.9, bf16[100,1024]{1,0:T(8,128)(2,1)} %w_out_in.1, s32[3,2048]{1,0:T(4,128)} %bitcast.5, ...), custom_call_target="tpu_custom_call" | custom-call | tf_op jit(solution)/shard_map/pallas_call | solution.py:447
  90.8 1.9 %copy.16 = f32[128,1024]{1,0:T(8,128)} copy(f32[128,1024]{1,0:T(8,128)} %get-tuple-element.16) | data formatting | bytes 1048576
  92.7 1.8 %copy.17 = f32[100,1024]{1,0:T(8,128)} copy(f32[100,1024]{1,0:T(8,128)} %get-tuple-element.17) | data formatting | bytes 819200
  94.5 1.3 %copy.18 = f32[1024]{0:T(1024)} copy(f32[1024]{0:T(1024)} %bitcast.8) | data formatting | bytes 8192

commit v3 on v2

--- a/solution.py
+++ b/solution.py
@@ -18,7 +18,7 @@
 def decoder(
     n_member, n_region, variables,
     latent, w_node, bias, w_out_in, src_t, weight_t, target, area,
-    grad_node, grad_out, grad_bias, loss_out,
+    node_out, head_out, loss_out,
     w_out, tail, ext, proj, adj, adj_t, hid, slope, preds, dpr, acc, gout, lacc, cb,
     part, recv_c, sum_c, recv_1a, recv_1b, sum_1a, sum_1b, recv_2, sum_2, recv_z, ob, lbuf,
     halo_s, halo_r, relay_s, relay_r, pa_s, pa_r, pb_s, pb_r, pf_s, pf_r,
@@ -380,16 +380,15 @@
         return pl.ds(pl.multiple_of(((mm % 2) * 2 + mm // 2) * quarter, quarter), quarter)
 
     def place_top(k, mm):
-        grad_node[:, columns(mm)] = ob[k, 0:rb, :].astype(F32)
+        node_out[:, columns(mm)] = ob[k, 0:rb, :]
 
     def place_low(k, mm):
-        grad_out[:, columns(mm)] = ob[k, rb : rb + vp, :].astype(F32)[0:variables]
-        grad_bias[:, columns(mm)] = ob[k, rb + vp : rb + vp + 16, :].astype(F32)[0:1]
+        head_out[:, columns(mm)] = ob[k, rb : rb + vp + 16, :]
 
     place_top(0, m)
     for copy in sharing:
         copy.wait_recv()
-    loss_out[0] = jnp.max((lbuf[0] + lbuf[1]) + (lbuf[2] + lbuf[3]))
+    loss_out[...] = (lbuf[0] + lbuf[1]) + (lbuf[2] + lbuf[3])
     for copy in h_copies:
         copy.wait_recv()
     b_y.start()
@@ -426,12 +425,19 @@
         copy.wait_send()
 
 
+def widen(variables, vp, node_half, head_half, loss_sum, grad_node, grad_out, grad_bias, loss):
+    grad_node[...] = node_half[...].astype(F32)
+    grad_out[...] = head_half[0:vp, :].astype(F32)[0:variables]
+    grad_bias[...] = head_half[vp : vp + 16, :].astype(F32)[0:1]
+    loss[0] = jnp.max(loss_sum[...])
+
+
 def local(n_member, n_region, latent, w_node, bias, w_out, edge_src, edge_weight, target, area):
     here, nodes, width = latent.shape
     points, fanout = edge_src.shape
     variables = target.shape[0]
     vp = -(-variables // 16) * 16
-    gc = 256
+    gc = 512
     chunks = points // gc
     span = 3 * nodes
     wide = span + 16
@@ -444,17 +450,15 @@
     grow = max(head, vp + 16)
     dma = lambda k: pltpu.SemaphoreType.DMA((k,))
     vm = lambda shape, t: pltpu.VMEM(shape, t)
-    grad_node, grad_out, grad_bias, loss = pl.pallas_call(
+    node_half, head_half, loss_sum = pl.pallas_call(
         functools.partial(decoder, n_member, n_region, variables),
         out_shape=(
-            jax.ShapeDtypeStruct((rb, width), F32),
-            jax.ShapeDtypeStruct((variables, width), F32),
-            jax.ShapeDtypeStruct((1, width), F32),
-            jax.ShapeDtypeStruct((1,), F32),
+            jax.ShapeDtypeStruct((rb, width), BF),
+            jax.ShapeDtypeStruct((vp + 16, width), BF),
+            jax.ShapeDtypeStruct((8, 128), F32),
         ),
         in_specs=[pl.BlockSpec(memory_space=pltpu.VMEM)] * 8,
-        out_specs=[pl.BlockSpec(memory_space=pltpu.VMEM)] * 3
-        + [pl.BlockSpec(memory_space=pltpu.SMEM)],
+        out_specs=[pl.BlockSpec(memory_space=pltpu.VMEM)] * 3,
         scratch_shapes=[
             vm((vp, width), BF),
             vm((16, points), F32),
@@ -494,6 +498,18 @@
         latent, w_node, bias.reshape(1, width), w_out, edge_src.T, edge_weight.T, target,
         area.reshape(1, points),
     )
+    grad_node, grad_out, grad_bias, loss = pl.pallas_call(
+        functools.partial(widen, variables, vp),
+        out_shape=(
+            jax.ShapeDtypeStruct((rb, width), F32),
+            jax.ShapeDtypeStruct((variables, width), F32),
+            jax.ShapeDtypeStruct((1, width), F32),
+            jax.ShapeDtypeStruct((1,), F32),
+        ),
+        in_specs=[pl.BlockSpec(memory_space=pltpu.VMEM)] * 3,
+        out_specs=[pl.BlockSpec(memory_space=pltpu.VMEM)] * 3
+        + [pl.BlockSpec(memory_space=pltpu.SMEM)],
+    )(node_half, head_half, loss_sum)
     return (grad_node, grad_out, grad_bias.reshape(width), loss)
 
 

time: 97.9 us -> 91.8 us (0.938)
  local copies, waits for them, and re-layouts: 4.94 us -> 0 us
  between operations: 2.45 us -> 0.64 us
    unnamed x3 -> x0, local copies, waits for them, and re-layouts: 4.94 us -> none
    pallas_call x0 -> x1, Pallas kernels: none -> 2.01 us  [local(): pl.pallas_call(functools.partial(widen, variables, vp), out_shape=(jax.Sh...]
    pallas_call x1, Pallas kernels: 90.2 us -> 89 us  [local(): pl.pallas_call(functools.partial(decoder, n_member, n_region, variables),...]
where the time goes in v3:
time: 91.8 us; the launch traced here: 91.7 us
  Pallas kernels  91 us (99%)
    pallas_call x1, Pallas kernels, local(): pl.pallas_call(functools.partial(decoder, n_member, n_region, variables),...  89 us
    pallas_call x1, Pallas kernels, local(): pl.pallas_call(functools.partial(widen, variables, vp), out_shape=(jax.Sh...  2.01 us

profile of v3, /device:TPU:0, one launch (start us, length us, event | category | flops | bytes accessed | tf_op | source)
XLA Modules:
  0.0 91.7 jit_solution(12252476794803761095)
XLA Ops:
  0.6 89.0 %shard_map.111 = (bf16[128,1024]{1,0:T(8,128)(2,1)}, bf16[128,1024]{1,0:T(8,128)(2,1)}, f32[8,128]{1,0:T(8,128)}) custom-call(bf16[2,128,1024]{2,1,0:T(8,128)(2,1)} %latent.1, bf16[1024,1024]{1,0:T(8,128)(2,1)} %w_node.1, f32[1,1024]{1,0:T(1,128)} %bitcast.8, bf16[100,1024]{1,0:T(8,128)(2,1)} %w_out_in.1, s32[3,2048]{1,0:T(4,128)} %bitcast.5, ...), custom_call_target="tpu_custom_call" | custom-call | tf_op jit(solution)/shard_map/pallas_call | solution.py:453
  89.6 2.0 %shard_map.112 = (f32[128,1024]{1,0:T(8,128)}, f32[100,1024]{1,0:T(8,128)}, f32[1,1024]{1,0:T(1,128)}, f32[1]{0:T(128)}) custom-call(bf16[128,1024]{1,0:T(8,128)(2,1)} %get-tuple-element.11.node_half, bf16[128,1024]{1,0:T(8,128)(2,1)} %get-tuple-element.12.head_half, f32[8,128]{1,0:T(8,128)} %get-tuple-element.13.loss_sum), custom_call_target="tpu_custom_call" | custom-call | tf_op jit(solution)/shard_map/pallas_call | solution.py:501

commit v4 on v3

--- a/solution.py
+++ b/solution.py
@@ -182,11 +182,6 @@
 
     def backward(c, _):
         rows = pl.ds(pl.multiple_of(c * gc, gc), gc)
-
-        @pl.when(c < lag)
-        def _():
-            to_y(steps - lag + c).wait_recv()
-            pass_on(steps - lag + c).start()
 
         for a in range(here):
             to_core(a * chunks + c).wait_recv()
@@ -233,6 +228,12 @@
             )
             dpre = (dh * slope[a, rows, :].astype(F32)).astype(BF)
             acc[a] += jnp.dot(adj_t[c], dpre, preferred_element_type=F32)
+
+        @pl.when(c < lag)
+        def _():
+            to_y(steps - lag + c).wait_recv()
+            pass_on(steps - lag + c).start()
+
         return 0
 
     lax.fori_loop(0, chunks, backward, 0)

time: 91.8 us -> 90 us (0.980)
  Pallas kernels: 91 us -> 89.2 us
    pallas_call x1, Pallas kernels: 89 us -> 87.2 us  [local(): pl.pallas_call(functools.partial(decoder, n_member, n_region, variables),...]
where the time goes in v4:
time: 90 us; the launch traced here: 89.8 us
  Pallas kernels  89.2 us (99%)
    pallas_call x1, Pallas kernels, local(): pl.pallas_call(functools.partial(decoder, n_member, n_region, variables),...  87.2 us
    pallas_call x1, Pallas kernels, local(): pl.pallas_call(functools.partial(widen, variables, vp), out_shape=(jax.Sh...  2.01 us

profile of v4, /device:TPU:0, one launch (start us, length us, event | category | flops | bytes accessed | tf_op | source)
XLA Modules:
  0.0 89.8 jit_solution(11237403792888253594)
XLA Ops:
  0.6 87.2 %shard_map.111 = (bf16[128,1024]{1,0:T(8,128)(2,1)}, bf16[128,1024]{1,0:T(8,128)(2,1)}, f32[8,128]{1,0:T(8,128)}) custom-call(bf16[2,128,1024]{2,1,0:T(8,128)(2,1)} %latent.1, bf16[1024,1024]{1,0:T(8,128)(2,1)} %w_node.1, f32[1,1024]{1,0:T(1,128)} %bitcast.8, bf16[100,1024]{1,0:T(8,128)(2,1)} %w_out_in.1, s32[3,2048]{1,0:T(4,128)} %bitcast.5, ...), custom_call_target="tpu_custom_call" | custom-call | tf_op jit(solution)/shard_map/pallas_call | solution.py:454
  87.8 2.0 %shard_map.112 = (f32[128,1024]{1,0:T(8,128)}, f32[100,1024]{1,0:T(8,128)}, f32[1,1024]{1,0:T(1,128)}, f32[1]{0:T(128)}) custom-call(bf16[128,1024]{1,0:T(8,128)(2,1)} %get-tuple-element.11.node_half, bf16[128,1024]{1,0:T(8,128)(2,1)} %get-tuple-element.12.head_half, f32[8,128]{1,0:T(8,128)} %get-tuple-element.13.loss_sum), custom_call_target="tpu_custom_call" | custom-call | tf_op jit(solution)/shard_map/pallas_call | solution.py:502
